TPU v7x, 32 devices: a whole 2x2x4 slice. The times are simulated.
32 devices in a mesh: groups: 2 (over y), row: 4 (over z), col: 2 (over x), sub: 2 (over core).
Axes of the slice: x: 2, y: 2, z: 4, core: 2. Of those that a mesh axis runs over, the one named last changes fastest.
Arguments:
- query_acts: bfloat16 [64, 128, 4096], P(('groups', 'col', 'sub'), None, 'row'), parts along dimension 0, may hold values from -6 to 6
- query_grads: bfloat16 [64, 128, 4096], P(('groups', 'col', 'sub'), None, 'row'), parts along dimension 0, may hold values from -0.5390625 to 0.5390625
- proj_in: bfloat16 [4096, 128], P('row'), may hold values from -0.09375 to 0.09375
- proj_out: bfloat16 [4096, 128], P('row'), may hold values from -0.09375 to 0.09375
- inverse_gram: float32 [16384, 16384], P('row', ('col', 'sub')), may hold values from -0.01 to 2.01, as said below
- store_slab: bfloat16 [2048, 16384], P(('groups', 'col'), ('row', 'sub')), parts along dimension 0, may hold values from -0.046875 to 0.046875
Outputs:
- scores: float32 [64, 1024], P('groups', 'col'), parts along dimension 0
There are 2 independent parts, one for each index of `groups`. A program takes and returns all parts, laid end to end along the dimension named above; an argument that names none is the same for every part. Nothing has to cross between parts.
Inputs may be any that keep to these rules, and one draw needn't show every extreme that they name: inverse_gram is symmetric.
All inputs are finite; a program needn't handle non-finite values.
Results may differ from a plain program's by a relative error of at most 0.0029.
Values may be sent and summed in bfloat16 or wider, within the bound.
No kernel may reach another device: no remote copies, remote signals or barrier semaphores. Data moves between devices by JAX's collectives and lax.ppermute only.
A program may use at most 128 MiB of HBM per device.

v0:
```python
import jax
import jax.numpy as jnp
from jax import lax
from jax.sharding import PartitionSpec as P


def body(query_acts, query_grads, proj_in, proj_out, inverse_gram, store_slab):
    row_count = lax.axis_size("row")
    row_index = lax.axis_index("row")
    sub_index = lax.axis_index("sub")
    in_width = proj_in.shape[1]
    act_part = jnp.einsum("qtd,dk->qtk", query_acts, proj_in, preferred_element_type=jnp.float32)
    grad_part = jnp.einsum("qtd,dk->qtk", query_grads, proj_out, preferred_element_type=jnp.float32)
    store_width = store_slab.shape[1]
    row_block = in_width // row_count
    act_whole, grad_proj = lax.psum((act_part, grad_part), "row")
    act_proj = lax.dynamic_slice_in_dim(act_whole, row_index * row_block, row_block, 2)
    kron_part = jnp.einsum("qta,qtb->qab", act_proj, grad_proj, precision=lax.Precision.HIGHEST)
    kron_feats = lax.all_gather(kron_part, ("col", "sub"), axis=0, tiled=True)
    features_flat = kron_feats.reshape(kron_feats.shape[0], -1)
    precond_part = jnp.dot(features_flat, inverse_gram, precision=lax.Precision.HIGHEST)
    precond_block = lax.psum(precond_part, "row").astype(jnp.bfloat16)
    precond_full = lax.all_gather(precond_block, ("col", "sub"), axis=1, tiled=True)
    store_start = (row_index * lax.axis_size("sub") + sub_index) * store_width
    precond_mine = lax.dynamic_slice_in_dim(precond_full, store_start, store_width, 1)
    score_part = lax.dot_general(
        precond_mine, store_slab, (((1,), (1,)), ((), ())), preferred_element_type=jnp.float32
    )
    return lax.psum(score_part, ("row", "sub"))


def solution(mesh):
    return jax.shard_map(
        body,
        mesh=mesh,
        in_specs=(
            P(("groups", "col", "sub"), None, "row"),
            P(("groups", "col", "sub"), None, "row"),
            P("row", None),
            P("row", None),
            P("row", ("col", "sub")),
            P(("groups", "col"), ("row", "sub")),
        ),
        out_specs=P("groups", "col"),
        check_vma=False,
    )
```

profile of v0, /device:TPU:0, one launch (start us, length us, event | category | flops | bytes accessed | tf_op | source)
XLA Modules:
  0.0 229.2 jit_solution(5424113497208901070)
XLA Ops:
  6.5 0.0 copy-start
  6.5 0.0 copy-start.2
  6.5 0.0 all-reduce.7.cloned.1.call-start
  6.5 1.6 copy-done
  8.1 0.0 copy-start.1
  8.1 2.6 %fusion.3 = f32[8,128,128]{2,1,0:T(8,128)} fusion(bf16[8,128,1024]{2,1,0:T(8,128)(2,1)S(1)} %copy-done, bf16[1024,128]{1,0:T(8,128)(2,1)} %param.9), kind=kOutput, calls=%fused_computation.3 | convolution fusion | flops 268435456 | bytes 2883584 | tf_op jit(solution)/shard_map/qtd,dk->qtk/dot_general | solution.py:13
  10.7 0.0 copy-done.2
  10.7 0.0 copy-done.1
  10.7 1.6 fusion.5
  12.4 0.0 all-reduce.7.cloned.1.call-update
  12.4 0.0 all-gather.2.cloned.1.call-start
  12.5 55.0 %all-reduce.7.cloned.1.call-done = (f32[8,128,128]{2,1,0:T(8,128)}, f32[8,128,128]{1,2,0:T(8,128)}) async-done(((f32[8,128,128]{2,1,0:T(8,128)}, f32[8,128,128]{1,2,0:T(8,128)}), (f32[8,128,128]{2,1,0:T(8,128)}, f32[8,128,128]{1,2,0:T(8,128)})) %all-reduce.7.cloned.1.call-update) | async-done | bytes 1048592 | tf_op jit(solution)/shard_map/psum | solution.py:16
  67.4 1.7 fusion.9
  69.1 7.1 %all_gather.6 = f32[32,32,128]{2,1,0:T(8,128)S(1)} all-gather(f32[8,32,128]{2,1,0:T(8,128)S(1)} %fusion.9), channel_id=1, replica_groups=mesh['groups'=2,'row'=4,'col'=2,'sub'=2] {'col','sub'}, dimensions={0}, use_global_device_ids=true | all-gather | bytes 655360 | tf_op jit(solution)/shard_map/all_gather | solution.py:19
  76.2 43.6 %fusion = f32[32,4096]{1,0:T(8,128)S(1)} fusion(f32[4096,4096]{1,0:T(8,128)} %param.10, f32[4,8,32,128]{3,2,1,0:T(8,128)S(1)} %bitcast.15), kind=kOutput, calls=%fused_computation | convolution fusion | flops 6442450944 | bytes 68157440 | tf_op jit(solution)/shard_map/dot_general | solution.py:21
  119.8 29.4 %all-reduce.8 = bf16[32,4096]{1,0:T(8,128)(2,1)} all-reduce(f32[32,4096]{1,0:T(8,128)S(1)} %fusion), channel_id=1, replica_groups=mesh['groups'=2,'row'=4,'col'=2,'sub'=2] {'row'}, use_global_device_ids=true, to_apply=%region_2.0 | all-reduce | flops 131072 | bytes 786432 | tf_op jit(solution)/shard_map/psum | solution.py:22
  149.2 0.0 all-gather.2.cloned.1.call-update
  149.3 0.0 all-reduce.5.cloned.1.call-start
  149.3 15.0 %all-gather.2.cloned.1.call-done = bf16[32,16384]{1,0:T(8,128)(2,1)} async-done(((bf16[32,4096]{1,0:T(8,128)(2,1)}), bf16[32,16384]{1,0:T(8,128)(2,1)}) %all-gather.2.cloned.1.call-update) | async-done | bytes 1048592 | tf_op jit(solution)/shard_map/all_gather | solution.py:23
  164.4 3.0 %fusion.7 = f32[32,512]{1,0:T(8,128)} fusion(bf16[512,2048]{1,0:T(8,128)(2,1)} %param.11, bf16[32,16384]{1,0:T(8,128)(2,1)} %all-gather.2.cloned.1.call-done, s32[]{:T(128)S(6)} %select_n.7), kind=kOutput, calls=%fused_computation.7 | convolution fusion | flops 67108864 | bytes 2293764 | tf_op jit(solution)/shard_map/dot_general | solution.py:26
  167.4 0.0 all-reduce.5.cloned.1.call-update
  167.4 53.8 %all-reduce.5.cloned.1.call-done = f32[32,512]{1,0:T(8,128)} async-done(((f32[32,512]{1,0:T(8,128)}), f32[32,512]{1,0:T(8,128)}) %all-reduce.5.cloned.1.call-update) | async-done | bytes 65552 | tf_op jit(solution)/shard_map/psum | solution.py:29
  221.2 1.5 copy.17
Async XLA Ops:
  6.5 1.6 copy-start
  6.5 4.2 %copy-start.2 = (bf16[1024,128]{1,0:T(8,128)(2,1)S(1)}, bf16[1024,128]{1,0:T(8,128)(2,1)}, u32[]{:S(2)}) copy-start(bf16[1024,128]{1,0:T(8,128)(2,1)} %param.8) | copy-start | bytes 786436
  6.5 60.9 %all-reduce.7.cloned.1.call-start = ((), (), s32[]{:S(2)}) async-start(), calls=%async_computation.2 | async-start | bytes 2097152 | tf_op jit(solution)/shard_map/psum | solution.py:16
  8.1 2.6 %copy-start.1 = (bf16[8,128,1024]{2,1,0:T(8,128)(2,1)S(1)}, bf16[8,128,1024]{2,1,0:T(8,128)(2,1)}, u32[]{:S(2)}) copy-start(bf16[8,128,1024]{2,1,0:T(8,128)(2,1)} %param.6) | copy-start | bytes 6291460
  12.4 152.0 %all-gather.2.cloned.1.call-start = ((), (), s32[]{:S(2)}) async-start(), calls=%async_computation | async-start | bytes 1310720 | tf_op jit(solution)/shard_map/all_gather | solution.py:23
  149.3 71.9 %all-reduce.5.cloned.1.call-start = ((), (), s32[]{:S(2)}) async-start(), calls=%async_computation.1 | async-start | bytes 131072 | tf_op jit(solution)/shard_map/psum | solution.py:29
Sparse Core Ops, SparseCore 0:
  12.5 54.8 all-reduce.6
  149.4 14.9 all-gather.1
  167.6 53.5 all-reduce.4
where the time goes:
time: 229 us
  waiting for transfers between devices  124 us (54%)
  matrix products  52.5 us (23%)
  blocking collectives  36.5 us (16%)
  between operations  13.1 us (6%)
  local copies, waits for them, and re-layouts  3.07 us (1%)
    psum x1, waiting for transfers between devices, body(): act_whole, grad_proj = lax.psum((act_part, grad_part), 'row')  55 us
    psum x1, waiting for transfers between devices, body(): return lax.psum(score_part, ('row', 'sub'))  53.8 us
    dot_general x1, matrix products, body(): jnp.dot(features_flat, inverse_gram, precision=lax.Precision.HIGHEST)  43.6 us
    psum x1, blocking collectives, body(): precond_block = lax.psum(precond_part, 'row').astype(jnp.bfloat16)  29.4 us
    all_gather x1, waiting for transfers between devices, body(): lax.all_gather(precond_block, ('col', 'sub'), axis=1, tiled=True)  15 us
    all_gather x1, blocking collectives, body(): kron_feats = lax.all_gather(kron_part, ('col', 'sub'), axis=0, tiled=True)  7.14 us
  transfers between devices with their start and end apart: 3, of which 3 were waited for; matrix products, arithmetic and copies ran while one was open for 0% of the time, Pallas kernels for 0%

commit v1 on v0

v1 whole, which is shorter than its diff:
```python
import functools

import jax
import jax.numpy as jnp
from jax import lax
from jax.experimental import pallas as pl
from jax.experimental.pallas import tpu as pltpu
from jax.sharding import PartitionSpec as P

HIGHEST = lax.Precision.HIGHEST


def plain_body(query_acts, query_grads, proj_in, proj_out, inverse_gram, store_slab):
    row_count = lax.axis_size("row")
    row_index = lax.axis_index("row")
    sub_index = lax.axis_index("sub")
    in_width = proj_in.shape[1]
    act_part = jnp.einsum("qtd,dk->qtk", query_acts, proj_in, preferred_element_type=jnp.float32)
    grad_part = jnp.einsum("qtd,dk->qtk", query_grads, proj_out, preferred_element_type=jnp.float32)
    store_width = store_slab.shape[1]
    row_block = in_width // row_count
    act_whole, grad_proj = lax.psum((act_part, grad_part), "row")
    act_proj = lax.dynamic_slice_in_dim(act_whole, row_index * row_block, row_block, 2)
    kron_part = jnp.einsum("qta,qtb->qab", act_proj, grad_proj, precision=HIGHEST)
    kron_feats = lax.all_gather(kron_part, ("col", "sub"), axis=0, tiled=True)
    features_flat = kron_feats.reshape(kron_feats.shape[0], -1)
    precond_part = jnp.dot(features_flat, inverse_gram, precision=HIGHEST)
    precond_block = lax.psum(precond_part, "row").astype(jnp.bfloat16)
    precond_full = lax.all_gather(precond_block, ("col", "sub"), axis=1, tiled=True)
    store_start = (row_index * lax.axis_size("sub") + sub_index) * store_width
    precond_mine = lax.dynamic_slice_in_dim(precond_full, store_start, store_width, 1)
    score_part = lax.dot_general(
        precond_mine, store_slab, (((1,), (1,)), ((), ())), preferred_element_type=jnp.float32
    )
    return lax.psum(score_part, ("row", "sub"))


PAD = 8
SHIFT = 13.0
LOG2E = 1.4426950408889634
WHOLE = pl.BlockSpec(memory_space=pltpu.VMEM)
MIB = 2**20


def exponents(part):
    top = jnp.max(jnp.abs(part), axis=0, keepdims=True)
    return jnp.ceil(jnp.log(jnp.clip(top, 1e-30, 1e30)) * LOG2E)


def scaled(part, k):
    return part * jnp.exp2(SHIFT - k)


def restored(part, k):
    return part * jnp.exp2(k - SHIFT)


def project_kernel(row_ref, acts_ref, grads_ref, in_ref, out_proj_ref, out_ref):
    del row_ref
    count = acts_ref.shape[0] * acts_ref.shape[1]
    pairs = ((acts_ref, in_ref), (grads_ref, out_proj_ref))
    for i, (x_ref, w_ref) in enumerate(pairs):
        x = x_ref[...].reshape(count, x_ref.shape[2])
        part = jnp.dot(x, w_ref[...], preferred_element_type=jnp.float32)
        k = exponents(part)
        out_ref[0, i * count : (i + 1) * count] = scaled(part, k)
        out_ref[0, 2 * count + i * PAD : 2 * count + (i + 1) * PAD] = jnp.broadcast_to(k, (PAD, k.shape[1]))


def project(query_acts, query_grads, proj_in, proj_out, row_count, row_index):
    queries, tokens, width = query_acts.shape
    own = queries // row_count
    out_width = proj_in.shape[1]
    height = 2 * own * tokens + 2 * PAD
    pick = lambda k, row: (row[0] ^ k, 0, 0)
    full = lambda k, row: (0, 0)
    return pl.pallas_call(
        project_kernel,
        grid_spec=pltpu.PrefetchScalarGridSpec(
            num_scalar_prefetch=1,
            grid=(row_count,),
            in_specs=[
                pl.BlockSpec((own, tokens, width), pick),
                pl.BlockSpec((own, tokens, width), pick),
                pl.BlockSpec(proj_in.shape, full),
                pl.BlockSpec(proj_out.shape, full),
            ],
            out_specs=pl.BlockSpec((1, height, out_width), lambda k, row: (k, 0, 0)),
        ),
        out_shape=jax.ShapeDtypeStruct((row_count, height, out_width), jnp.float32),
        compiler_params=pltpu.CompilerParams(vmem_limit_bytes=16 * MIB),
        name="project",
    )(row_index.reshape(1), query_acts, query_grads, proj_in, proj_out)


def kron_kernel(place_ref, own_ref, *refs, tokens):
    out_ref = refs[-1]
    count = (own_ref.shape[0] - 2 * PAD) // 2
    sums = []
    for i in range(2):
        total = None
        for ref in (own_ref,) + refs[:-1]:
            k = 2 * count + i * PAD
            part = restored(ref[i * count : (i + 1) * count], ref[k : k + 1])
            total = part if total is None else total + part
        sums.append(total)
    acts, grads = sums
    height = acts.shape[1] // 8
    for j in range(count // tokens):
        rows = slice(j * tokens, (j + 1) * tokens)
        kron = lax.dot_general(
            acts[rows], grads[rows], (((0,), (0,)), ((), ())), precision=HIGHEST, preferred_element_type=jnp.float32
        )
        for c in range(2):
            for s in range(2):
                for g in range(2):
                    start = ((c * 2 + s) * 2 + g) * height
                    out_ref[g ^ place_ref[0], c ^ place_ref[2], s ^ place_ref[3], j * height : (j + 1) * height] = (
                        kron[start : start + height]
                    )


def pack_kernel(kept_ref, got_ref, out_ref):
    lanes = kept_ref.shape[-1]
    parts = jnp.concatenate([kept_ref[...].reshape(-1, lanes), got_ref[...].reshape(-1, lanes)], 0)
    k = exponents(parts)
    out_ref[: parts.shape[0]] = scaled(parts, k)
    out_ref[parts.shape[0] :] = jnp.broadcast_to(k, (PAD, lanes))


def split(block):
    high = block.astype(jnp.bfloat16)
    return high, (block - high.astype(jnp.float32)).astype(jnp.bfloat16)


def gram_split_kernel(place_ref, gram_ref, high_ref, low_ref, buffer, sems):
    slots, tile, width = buffer.shape
    steps = high_ref.shape[0] // tile
    column = pl.multiple_of(place_ref[0] * width, width)

    def copy(i):
        rows = pl.ds(pl.multiple_of(i * tile, tile), tile)
        slot = lax.rem(i, slots)
        return pltpu.make_async_copy(gram_ref.at[rows, pl.ds(column, width)], buffer.at[slot], sems.at[slot])

    for i in range(slots - 1):
        copy(i).start()

    @pl.loop(0, steps)
    def _(i):
        @pl.when(i + slots - 1 < steps)
        def _():
            copy(i + slots - 1).start()

        copy(i).wait()
        rows = pl.ds(pl.multiple_of(i * tile, tile), tile)
        high, low = split(buffer[lax.rem(i, slots)])
        high_ref[rows] = high
        low_ref[rows] = low


def gram_split(inverse_gram, place, tile=256, slots=4):
    rows, width = inverse_gram.shape
    half = width // 2
    tile = min(tile, rows)
    terms = pltpu.VMEM((rows, half), jnp.bfloat16)
    return pl.pallas_call(
        gram_split_kernel,
        in_specs=[pl.BlockSpec(memory_space=pltpu.SMEM), pl.BlockSpec(memory_space=pltpu.HBM)],
        out_specs=[WHOLE, WHOLE],
        out_shape=[terms, terms],
        scratch_shapes=[pltpu.VMEM((slots, tile, half), jnp.float32), pltpu.SemaphoreType.DMA((slots,))],
        compiler_params=pltpu.CompilerParams(vmem_limit_bytes=SPLIT_LIMIT),
        cost_estimate=pl.CostEstimate(flops=0, bytes_accessed=4 * rows * half, transcendentals=0),
        name="gram_split",
    )(place, inverse_gram)


def gram_kernel(place_ref, high_ref, low_ref, *refs, row_count, own):
    sources, (out_ref, natural, terms) = refs[:row_count], refs[row_count:]
    group, row, col, sub = (place_ref[i] for i in range(4))
    height, queries, lanes = natural.shape
    for z in range(row_count):
        count = sources[z].shape[0] - PAD
        piece = restored(sources[z][:count], sources[z][count : count + 1])
        for place in range(8):
            s, c, g = place // 4, place // 2 % 2, place % 2
            first = ((((g ^ group) * 2 + (c ^ col)) * 2 + (s ^ sub)) * row_count + (z ^ row)) * own
            for j in range(own):
                start = (place * own + j) * height
                natural[:, pl.ds(first + j, 1), :] = piece[start : start + height].reshape(height, 1, lanes)
    for a in range(height):
        high, low = split(natural[a])
        terms[:queries, a * lanes : (a + 1) * lanes] = high
        terms[queries:, a * lanes : (a + 1) * lanes] = low
    width = out_ref.shape[3]
    tile = min(TILE, width)
    dims = (((1,), (1,)), ((), ()))

    @pl.loop(0, 2 * width // tile)
    def _(i):
        rows = pl.ds(pl.multiple_of(i * tile, tile), tile)
        part = lax.dot_general(high_ref[rows], terms[...], dims, preferred_element_type=jnp.float32)
        part += lax.dot_general(low_ref[rows], terms[...], dims, preferred_element_type=jnp.float32)
        done = (part[:, :queries] + part[:, queries:]).T
        half = i // (width // tile)
        columns = pl.ds(pl.multiple_of((i - half * (width // tile)) * tile, tile), tile)
        for g in range(2):
            out_ref[half ^ sub, g ^ group, :, columns] = done[g * (queries // 2) : (g + 1) * (queries // 2)]


TILE = 512
SPLIT_LIMIT = 16 * MIB
PRODUCT_LIMIT = 16 * MIB


def gram_product(place, high, low, sources, own, tokens_width):
    rows, half = high.shape
    row_count = len(sources)
    queries = 8 * row_count * own
    return pl.pallas_call(
        functools.partial(gram_kernel, row_count=row_count, own=own),
        in_specs=[pl.BlockSpec(memory_space=pltpu.SMEM)] + [WHOLE] * (2 + row_count),
        out_specs=WHOLE,
        out_shape=jax.ShapeDtypeStruct((2, 2, queries // 2, rows // 2), jnp.float32),
        scratch_shapes=[
            pltpu.VMEM((half // tokens_width, queries, tokens_width), jnp.float32),
            pltpu.VMEM((2 * queries, half), jnp.bfloat16),
        ],
        compiler_params=pltpu.CompilerParams(vmem_limit_bytes=PRODUCT_LIMIT),
        cost_estimate=pl.CostEstimate(flops=8 * queries * rows * half, bytes_accessed=4 * rows * half, transcendentals=0),
        name="gram_product",
    )(place, high, low, *sources)


def others(pick, axis):
    size = lax.axis_size(axis)
    index = lax.axis_index(axis)
    return [lax.ppermute(pick(index ^ k), axis, [(i, i ^ k) for i in range(size)]) for k in range(1, size)]


def tree_sum(terms):
    while len(terms) > 1:
        terms = [terms[i] + terms[i + 1] for i in range(0, len(terms), 2)]
    return terms[0]


def swapped(array, axis):
    return others(lambda d: array, axis)[0]


def call(kernel, shape, name, *args):
    specs = [pl.BlockSpec(memory_space=pltpu.SMEM) if a.dtype == jnp.int32 else WHOLE for a in args]
    return pl.pallas_call(
        kernel,
        in_specs=specs,
        out_specs=WHOLE,
        out_shape=jax.ShapeDtypeStruct(shape, jnp.float32),
        compiler_params=pltpu.CompilerParams(vmem_limit_bytes=16 * MIB),
        name=name,
    )(*args)


def body(query_acts, query_grads, proj_in, proj_out, inverse_gram, store_slab):
    row_count = lax.axis_size("row")
    row_index = lax.axis_index("row")
    place = jnp.stack([lax.axis_index(axis) for axis in ("groups", "row", "col", "sub")])
    queries, tokens = query_acts.shape[:2]
    own = queries // row_count
    in_width, out_width = proj_in.shape[1], proj_out.shape[1]
    parts = project(query_acts, query_grads, proj_in, proj_out, row_count, row_index)
    wire = [parts[k].astype(jnp.float16) for k in range(1, row_count)]
    got = [
        lax.ppermute(wire[k - 1], "row", [(i, i ^ k) for i in range(row_count)]).astype(jnp.float32)
        for k in range(1, row_count)
    ]
    high, low = gram_split(inverse_gram, place)
    height = own * in_width // 8
    kron = call(
        functools.partial(kron_kernel, tokens=tokens), (2, 2, 2, height, out_width), "kron", place, parts[0], *got
    )
    near = jnp.stack([kron[0], swapped(kron[1], "groups")], 2)
    near = jnp.stack([near[0], swapped(near[1], "col")], 1)
    packed = call(pack_kernel, (8 * height + PAD, out_width), "pack", near[0], swapped(near[1], "sub"))
    wire = packed.astype(jnp.float16)
    sources = [packed] + [got.astype(jnp.float32) for got in others(lambda d: wire, "row")]
    part = gram_product(place, high, low, sources, own, out_width)
    total = part[0] + swapped(part[1], "sub")
    total = total[0] + swapped(total[1].astype(jnp.bfloat16), "groups").astype(jnp.float32)
    total = total + swapped(total.astype(jnp.bfloat16), "col").astype(jnp.float32)
    high = lax.reduce_precision(total, 8, 7)
    terms = jnp.concatenate([high, total - high], 0).astype(jnp.bfloat16)
    scores = lax.dot_general(
        terms, store_slab, (((1,), (1,)), ((), ())), preferred_element_type=jnp.float32
    )
    scores = scores[: total.shape[0]] + scores[total.shape[0] :]
    for axis in ("sub", "row"):
        scores = tree_sum([scores] + others(lambda d, sent=scores: sent, axis))
    return scores


def solution(mesh):
    shape = mesh.shape
    rows = shape["row"]
    paired = shape["groups"] == shape["col"] == shape["sub"] == 2 and rows & (rows - 1) == 0

    def chosen(query_acts, query_grads, proj_in, proj_out, *rest):
        queries = query_acts.shape[0] // (shape["groups"] * shape["col"] * shape["sub"])
        square = proj_in.shape[1] == proj_out.shape[1] == 128
        chosen_body = body if paired and square and queries % rows == 0 else plain_body
        return jax.shard_map(
            chosen_body,
            mesh=mesh,
            in_specs=(
                P(("groups", "col", "sub"), None, "row"),
                P(("groups", "col", "sub"), None, "row"),
                P("row", None),
                P("row", None),
                P("row", ("col", "sub")),
                P(("groups", "col"), ("row", "sub")),
            ),
            out_specs=P("groups", "col"),
            check_vma=False,
        )(query_acts, query_grads, proj_in, proj_out, *rest)

    return chosen
```

time: 229 us -> 88.5 us (0.39)
  waiting for transfers between devices: 124 us -> 32.4 us
  matrix products: 52.5 us -> 0.77 us
  blocking collectives: 36.5 us -> 0 us
  Pallas kernels: 0 us -> 27.2 us
  starting transfers between devices: 0.09 us -> 21.1 us
  between operations: 13.1 us -> 0.25 us
  local copies, waits for them, and re-layouts: 3.07 us -> 5.4 us
    psum x2 -> x0, waiting for transfers between devices: 109 us -> none  [the longest x1 55 us: body(): act_whole, grad_proj = lax.psum((act_part, grad_part), 'row')]
    dot_general x5 -> x1, matrix products: 52.5 us -> 0.77 us  [body(): lax.dot_general(terms, store_slab, (((1,), (1,)), ((), ())), preferred_el...]
    ppermute x0 -> x16, waiting for transfers between devices: none -> 32.4 us  [the longest x13 21.8 us: others(): lax.ppermute(pick(index ^ k), axis, [(i, i ^ k) for i in range(size)])]
    psum x1 -> x0, blocking collectives: 29.4 us -> none  [body(): precond_block = lax.psum(precond_part, 'row').astype(jnp.bfloat16)]
    pallas_call x0 -> x5, Pallas kernels: none -> 27.2 us  [the longest x1 12.7 us: gram_product(): pl.pallas_call(functools.partial(gram_kernel, row_count=row_count, own=ow...]
    ppermute x0 -> x16, starting transfers between devices: none -> 21.1 us  [the longest x13 15.4 us: others(): lax.ppermute(pick(index ^ k), axis, [(i, i ^ k) for i in range(size)])]
    all_gather x1 -> x0, waiting for transfers between devices: 15 us -> none  [body(): lax.all_gather(precond_block, ('col', 'sub'), axis=1, tiled=True)]
    all_gather x1 -> x0, blocking collectives: 7.14 us -> none  [body(): kron_feats = lax.all_gather(kron_part, ('col', 'sub'), axis=0, tiled=True)]
  transfers between devices with their start and end apart: 3 -> 16, of which waited for: 3 -> 11; matrix products, arithmetic and copies ran while one was open for 0% -> 0% of each run, Pallas kernels for 0% -> 13%
where the time goes in v1:
time: 88.5 us; the launch traced here: 88.3 us
  waiting for transfers between devices  32.4 us (37%)
  Pallas kernels  27.2 us (31%)
  starting transfers between devices  21.1 us (24%)
  local copies, waits for them, and re-layouts  5.4 us (6%)
  other arithmetic  1.11 us (1%)
    ppermute x13, waiting for transfers between devices, others(): lax.ppermute(pick(index ^ k), axis, [(i, i ^ k) for i in range(size)])  21.8 us
    ppermute x13, starting transfers between devices, others(): lax.ppermute(pick(index ^ k), axis, [(i, i ^ k) for i in range(size)])  15.4 us
    pallas_call x1, Pallas kernels, gram_product(): pl.pallas_call(functools.partial(gram_kernel, row_count=row_count, own=ow...  12.7 us
    pallas_call x1, Pallas kernels, gram_split(): pl.pallas_call(gram_split_kernel, in_specs=[pl.BlockSpec(memory_space=plt...  11.7 us
    ppermute x3, waiting for transfers between devices, body(): lax.ppermute(wire[k - 1], 'row', [(i, i ^ k) for i in range(row_count)])  10.7 us
    ppermute x3, starting transfers between devices, body(): lax.ppermute(wire[k - 1], 'row', [(i, i ^ k) for i in range(row_count)])  5.75 us
    unnamed x10, local copies, waits for them, and re-layouts  5.23 us
    pallas_call x1, Pallas kernels, project(): pl.pallas_call(project_kernel, grid_spec=pltpu.PrefetchScalarGridSpec(num...  1.86 us
  transfers between devices with their start and end apart: 16, of which 11 were waited for; matrix products, arithmetic and copies ran while one was open for 0% of the time, Pallas kernels for 13%

profile of v1, /device:TPU:0, one launch (start us, length us, event | category | flops | bytes accessed | tf_op | source)
XLA Modules:
  0.0 88.3 jit_solution(16323071212798549584)
XLA Ops:
  0.0 1.7 %copy-done.1 = bf16[8,128,1024]{2,1,0:T(8,128)(2,1)S(1)} copy-done((bf16[8,128,1024]{2,1,0:T(8,128)(2,1)S(1)}, bf16[8,128,1024]{2,1,0:T(8,128)(2,1)}, u32[]{:S(2)}) %copy-start.1) | copy-done | bytes 2097176
  1.7 1.6 %copy-done.2 = bf16[8,128,1024]{2,1,0:T(8,128)(2,1)S(1)} copy-done((bf16[8,128,1024]{2,1,0:T(8,128)(2,1)S(1)}, bf16[8,128,1024]{2,1,0:T(8,128)(2,1)}, u32[]{:S(2)}) %copy-start.2) | copy-done | bytes 2097176
  5.2 1.9 %project.1 = f32[4,528,128]{2,1,0:T(8,128)S(1)} custom-call(s32[1]{0:T(128)} %bitcast.1.row_ref, bf16[8,128,1024]{2,1,0:T(8,128)(2,1)S(1)} %copy-done.1, bf16[8,128,1024]{2,1,0:T(8,128)(2,1)S(1)} %copy-done.2, bf16[1024,128]{1,0:T(8,128)(2,1)S(1)} %copy-done.3, bf16[1024,128]{1,0:T(8,128)(2,1)S(1)} %copy-done.4), custom_call_target="tpu_custom_call" | custom-call | tf_op jit(solution)/shard_map/project/pallas_call | solution.py:77
  7.3 5.1 %collective-permute-start.2 = (f16[528,128]{1,0:T(8,128)(2,1)S(1)}, f16[528,128]{1,0:T(8,128)(2,1)S(1)}, u32[]{:S(2)}, u32[]{:S(2)}) collective-permute-start(f16[528,128]{1,0:T(8,128)(2,1)S(1)} %get-tuple-element.11), channel_id=1, source_target_pairs={{0,12},{4,8},{8,4},{12,0},{1,13},{5,9},{9,5},{13,1},{2,14},{6,10},... | collective-permute-start | bytes 405512 | tf_op jit(solution)/shard_map/ppermute | solution.py:274
  13.1 3.8 %collective-permute-done.2 = f16[528,128]{1,0:T(8,128)(2,1)S(1)} collective-permute-done((f16[528,128]{1,0:T(8,128)(2,1)S(1)}, f16[528,128]{1,0:T(8,128)(2,1)S(1)}, u32[]{:S(2)}, u32[]{:S(2)}) %collective-permute-start.2) | collective-permute-done | bytes 135200 | tf_op jit(solution)/shard_map/ppermute | solution.py:274
  16.9 6.9 %collective-permute-done.1 = f16[528,128]{1,0:T(8,128)(2,1)S(1)} collective-permute-done((f16[528,128]{1,0:T(8,128)(2,1)S(1)}, f16[528,128]{1,0:T(8,128)(2,1)S(1)}, u32[]{:S(2)}, u32[]{:S(2)}) %collective-permute-start.1) | collective-permute-done | bytes 135200 | tf_op jit(solution)/shard_map/ppermute | solution.py:274
  24.8 1.6 %collective-permute-start.3 = (f32[2,2,32,128]{3,2,1,0:T(8,128)S(1)}, f32[2,2,32,128]{3,2,1,0:T(8,128)S(1)}, u32[]{:S(2)}, u32[]{:S(2)}) collective-permute-start(f32[2,2,32,128]{3,2,1,0:T(8,128)S(1)} %get-tuple-element.18), channel_id=1, source_target_pairs={{0,16},{16,0},{1,17},{17,1},{2,18},{18,2},{3,19},{19,3},{4,20},{20... | collective-permute-start | bytes 196616 | tf_op jit(solution)/shard_map/ppermute | solution.py:239
  26.4 2.7 %collective-permute-done.3 = f32[2,2,32,128]{3,2,1,0:T(8,128)S(1)} collective-permute-done((f32[2,2,32,128]{3,2,1,0:T(8,128)S(1)}, f32[2,2,32,128]{3,2,1,0:T(8,128)S(1)}, u32[]{:S(2)}, u32[]{:S(2)}) %collective-permute-start.3) | collective-permute-done | bytes 65568 | tf_op jit(solution)/shard_map/ppermute | solution.py:239
  29.1 1.6 %collective-permute-start.4 = (f32[2,2,32,128]{3,2,1,0:T(8,128)S(1)}, f32[2,2,32,128]{3,2,1,0:T(8,128)S(1)}, u32[]{:S(2)}, u32[]{:S(2)}) collective-permute-start(f32[2,2,32,128]{3,2,1,0:T(8,128)S(1)} %get-tuple-element.16), channel_id=1, source_target_pairs={{0,2},{2,0},{1,3},{3,1},{4,6},{6,4},{5,7},{7,5},{8,10},{10,8},{9,1... | collective-permute-start | bytes 196616 | tf_op jit(solution)/shard_map/ppermute | solution.py:239
  30.7 2.8 %collective-permute-done.4 = f32[2,2,32,128]{3,2,1,0:T(8,128)S(1)} collective-permute-done((f32[2,2,32,128]{3,2,1,0:T(8,128)S(1)}, f32[2,2,32,128]{3,2,1,0:T(8,128)S(1)}, u32[]{:S(2)}, u32[]{:S(2)}) %collective-permute-start.4) | collective-permute-done | bytes 65568 | tf_op jit(solution)/shard_map/ppermute | solution.py:239
  33.6 1.2 %collective-permute-done.5.got_ref = f32[2,2,32,128]{3,2,1,0:T(8,128)S(1)} collective-permute-done((f32[2,2,32,128]{3,2,1,0:T(8,128)S(1)}, f32[2,2,32,128]{3,2,1,0:T(8,128)S(1)}, u32[]{:S(2)}, u32[]{:S(2)}) %collective-permute-start.5) | collective-permute-done | bytes 65568 | tf_op jit(solution)/shard_map/ppermute | solution.py:239
  34.9 2.6 %collective-permute-start.8 = (f16[264,128]{1,0:T(8,128)(2,1)S(1)}, f16[264,128]{1,0:T(8,128)(2,1)S(1)}, u32[]{:S(2)}, u32[]{:S(2)}) collective-permute-start(f16[264,128]{1,0:T(8,128)(2,1)S(1)} %convert_element_type.53), channel_id=1, source_target_pairs={{0,12},{4,8},{8,4},{12,0},{1,13},{5,9},{9,5},{13,1},{2,14},{6,10},... | collective-permute-start | bytes 202760 | tf_op jit(solution)/shard_map/ppermute | solution.py:239
  37.4 1.9 %collective-permute-start.6 = (f16[264,128]{1,0:T(8,128)(2,1)S(1)}, f16[264,128]{1,0:T(8,128)(2,1)S(1)}, u32[]{:S(2)}, u32[]{:S(2)}) collective-permute-start(f16[264,128]{1,0:T(8,128)(2,1)S(1)} %convert_element_type.53), channel_id=1, source_target_pairs={{0,4},{4,0},{8,12},{12,8},{1,5},{5,1},{9,13},{13,9},{2,6},{6,2},{1... | collective-permute-start | bytes 202760 | tf_op jit(solution)/shard_map/ppermute | solution.py:239
  39.3 11.7 %gram_split.1 = (bf16[4096,2048]{1,0:T(8,128)(2,1)S(1)}, bf16[4096,2048]{1,0:T(8,128)(2,1)S(1)}) custom-call(s32[4]{0:T(128)S(1)} %pad_add_fusion.place_ref, f32[4096,4096]{1,0:T(8,128)} %gram_ref.1), custom_call_target="tpu_custom_call" | custom-call | bytes 33554432 | tf_op jit(solution)/shard_map/gram_split/pallas_call | solution.py:167
  51.2 12.7 %gram_product.1 = f32[2,2,32,2048]{3,2,1,0:T(8,128)S(1)} custom-call(s32[4]{0:T(128)S(1)} %pad_add_fusion.place_ref, bf16[4096,2048]{1,0:T(8,128)(2,1)S(1)} %get-tuple-element.7.high_ref, bf16[4096,2048]{1,0:T(8,128)(2,1)S(1)} %get-tuple-element.8.low_ref, f32[264,128]{1,0:T(8,128)S(1)} %pack.1.refs_0_, f32[264,128]{1,0:T(8,128)S(1)} %convert_element_type.54.refs_1_, ...), custom_call_target="tpu_custom_call" | custom-call | flops 4294967296 | bytes 33554432 | tf_op jit(solution)/shard_map/gram_product/pallas_call | solution.py:221
  63.9 1.9 %collective-permute-done.9 = f32[2,32,2048]{2,1,0:T(8,128)S(1)} collective-permute-done((f32[2,32,2048]{2,1,0:T(8,128)S(1)}, f32[2,32,2048]{2,1,0:T(8,128)S(1)}, u32[]{:S(2)}, u32[]{:S(2)}) %collective-permute-start.9) | collective-permute-done | bytes 524320 | tf_op jit(solution)/shard_map/ppermute | solution.py:239
  65.9 1.6 %collective-permute-start.10 = (bf16[32,2048]{1,0:T(8,128)(2,1)S(1)}, bf16[32,2048]{1,0:T(8,128)(2,1)S(1)}, u32[]{:S(2)}, u32[]{:S(2)}) collective-permute-start(bf16[32,2048]{1,0:T(8,128)(2,1)S(1)} %fusion.7), channel_id=1, source_target_pairs={{0,16},{16,0},{1,17},{17,1},{2,18},{18,2},{3,19},{19,3},{4,20},{20... | collective-permute-start | bytes 393224 | tf_op jit(solution)/shard_map/ppermute | solution.py:239
  67.5 4.0 %collective-permute-done.10 = bf16[32,2048]{1,0:T(8,128)(2,1)S(1)} collective-permute-done((bf16[32,2048]{1,0:T(8,128)(2,1)S(1)}, bf16[32,2048]{1,0:T(8,128)(2,1)S(1)}, u32[]{:S(2)}, u32[]{:S(2)}) %collective-permute-start.10) | collective-permute-done | bytes 131104 | tf_op jit(solution)/shard_map/ppermute | solution.py:239
  71.6 1.6 %collective-permute-start.11 = (bf16[32,2048]{1,0:T(8,128)(2,1)S(1)}, bf16[32,2048]{1,0:T(8,128)(2,1)S(1)}, u32[]{:S(2)}, u32[]{:S(2)}) collective-permute-start(bf16[32,2048]{1,0:T(8,128)(2,1)S(1)} %fusion.8), channel_id=1, source_target_pairs={{0,2},{2,0},{1,3},{3,1},{4,6},{6,4},{5,7},{7,5},{8,10},{10,8},{9,1... | collective-permute-start | bytes 393224 | tf_op jit(solution)/shard_map/ppermute | solution.py:239
  73.1 3.5 %collective-permute-done.11 = bf16[32,2048]{1,0:T(8,128)(2,1)S(1)} collective-permute-done((bf16[32,2048]{1,0:T(8,128)(2,1)S(1)}, bf16[32,2048]{1,0:T(8,128)(2,1)S(1)}, u32[]{:S(2)}, u32[]{:S(2)}) %collective-permute-start.11) | collective-permute-done | bytes 131104 | tf_op jit(solution)/shard_map/ppermute | solution.py:239
  78.8 2.5 %collective-permute-start.15 = (f32[32,512]{1,0:T(8,128)S(1)}, f32[32,512]{1,0:T(8,128)S(1)}, u32[]{:S(2)}, u32[]{:S(2)}) collective-permute-start(f32[32,512]{1,0:T(8,128)S(1)} %fusion.17), channel_id=1, source_target_pairs={{0,12},{4,8},{8,4},{12,0},{1,13},{5,9},{9,5},{13,1},{2,14},{6,10},... | collective-permute-start | bytes 196616 | tf_op jit(solution)/shard_map/ppermute | solution.py:239
  81.3 1.9 %collective-permute-start.13 = (f32[32,512]{1,0:T(8,128)S(1)}, f32[32,512]{1,0:T(8,128)S(1)}, u32[]{:S(2)}, u32[]{:S(2)}) collective-permute-start(f32[32,512]{1,0:T(8,128)S(1)} %fusion.17), channel_id=1, source_target_pairs={{0,4},{4,0},{8,12},{12,8},{1,5},{5,1},{9,13},{13,9},{2,6},{6,2},{1... | collective-permute-start | bytes 196616 | tf_op jit(solution)/shard_map/ppermute | solution.py:239
  83.2 2.4 %collective-permute-done.15 = f32[32,512]{1,0:T(8,128)S(1)} collective-permute-done((f32[32,512]{1,0:T(8,128)S(1)}, f32[32,512]{1,0:T(8,128)S(1)}, u32[]{:S(2)}, u32[]{:S(2)}) %collective-permute-start.15) | collective-permute-done | bytes 65568 | tf_op jit(solution)/shard_map/ppermute | solution.py:239
  85.6 2.0 %collective-permute-done.14 = f32[32,512]{1,0:T(8,128)S(1)} collective-permute-done((f32[32,512]{1,0:T(8,128)S(1)}, f32[32,512]{1,0:T(8,128)S(1)}, u32[]{:S(2)}, u32[]{:S(2)}) %collective-permute-start.14) | collective-permute-done | bytes 65568 | tf_op jit(solution)/shard_map/ppermute | solution.py:239
  (46 shorter events, 7.0 us)
Async XLA Ops:
  0.0 76.7 %copy-start = (bf16[512,2048]{1,0:T(8,128)(2,1)S(1)}, bf16[512,2048]{1,0:T(8,128)(2,1)}, u32[]{:S(2)}) copy-start(bf16[512,2048]{1,0:T(8,128)(2,1)} %param.11) | copy-start | bytes 6291460
  0.0 1.7 %copy-start.1 = (bf16[8,128,1024]{2,1,0:T(8,128)(2,1)S(1)}, bf16[8,128,1024]{2,1,0:T(8,128)(2,1)}, u32[]{:S(2)}) copy-start(bf16[8,128,1024]{2,1,0:T(8,128)(2,1)} %acts_ref.1) | copy-start | bytes 6291460
  1.7 1.6 %copy-start.2 = (bf16[8,128,1024]{2,1,0:T(8,128)(2,1)S(1)}, bf16[8,128,1024]{2,1,0:T(8,128)(2,1)}, u32[]{:S(2)}) copy-start(bf16[8,128,1024]{2,1,0:T(8,128)(2,1)} %grads_ref.1) | copy-start | bytes 6291460
  3.3 0.9 %copy-start.3 = (bf16[1024,128]{1,0:T(8,128)(2,1)S(1)}, bf16[1024,128]{1,0:T(8,128)(2,1)}, u32[]{:S(2)}) copy-start(bf16[1024,128]{1,0:T(8,128)(2,1)} %in_ref.1) | copy-start | bytes 786436
  4.3 0.9 %copy-start.4 = (bf16[1024,128]{1,0:T(8,128)(2,1)S(1)}, bf16[1024,128]{1,0:T(8,128)(2,1)}, u32[]{:S(2)}) copy-start(bf16[1024,128]{1,0:T(8,128)(2,1)} %out_proj_ref.1) | copy-start | bytes 786436
  7.3 9.6 %collective-permute-start.2 = (f16[528,128]{1,0:T(8,128)(2,1)S(1)}, f16[528,128]{1,0:T(8,128)(2,1)S(1)}, u32[]{:S(2)}, u32[]{:S(2)}) collective-permute-start(f16[528,128]{1,0:T(8,128)(2,1)S(1)} %get-tuple-element.11), channel_id=1, source_target_pairs={{0,12},{4,8},{8,4},{12,0},{1,13},{5,9},{9,5},{13,1},{2,14},{6,10},... | collective-permute-start | bytes 405512 | tf_op jit(solution)/shard_map/ppermute | solution.py:274
  12.4 11.4 %collective-permute-start.1 = (f16[528,128]{1,0:T(8,128)(2,1)S(1)}, f16[528,128]{1,0:T(8,128)(2,1)S(1)}, u32[]{:S(2)}, u32[]{:S(2)}) collective-permute-start(f16[528,128]{1,0:T(8,128)(2,1)S(1)} %get-tuple-element.12), channel_id=1, source_target_pairs={{0,8},{4,12},{8,0},{12,4},{1,9},{5,13},{9,1},{13,5},{2,10},{6,14},... | collective-permute-start | bytes 405512 | tf_op jit(solution)/shard_map/ppermute | solution.py:274
  12.4 11.4 %collective-permute-start = (f16[528,128]{1,0:T(8,128)(2,1)S(1)}, f16[528,128]{1,0:T(8,128)(2,1)S(1)}, u32[]{:S(2)}, u32[]{:S(2)}) collective-permute-start(f16[528,128]{1,0:T(8,128)(2,1)S(1)} %get-tuple-element.13), channel_id=1, source_target_pairs={{0,4},{4,0},{8,12},{12,8},{1,5},{5,1},{9,13},{13,9},{2,6},{6,2},{1... | collective-permute-start | bytes 405512 | tf_op jit(solution)/shard_map/ppermute | solution.py:274
  24.8 4.3 %collective-permute-start.3 = (f32[2,2,32,128]{3,2,1,0:T(8,128)S(1)}, f32[2,2,32,128]{3,2,1,0:T(8,128)S(1)}, u32[]{:S(2)}, u32[]{:S(2)}) collective-permute-start(f32[2,2,32,128]{3,2,1,0:T(8,128)S(1)} %get-tuple-element.18), channel_id=1, source_target_pairs={{0,16},{16,0},{1,17},{17,1},{2,18},{18,2},{3,19},{19,3},{4,20},{20... | collective-permute-start | bytes 196616 | tf_op jit(solution)/shard_map/ppermute | solution.py:239
  29.1 4.3 %collective-permute-start.4 = (f32[2,2,32,128]{3,2,1,0:T(8,128)S(1)}, f32[2,2,32,128]{3,2,1,0:T(8,128)S(1)}, u32[]{:S(2)}, u32[]{:S(2)}) collective-permute-start(f32[2,2,32,128]{3,2,1,0:T(8,128)S(1)} %get-tuple-element.16), channel_id=1, source_target_pairs={{0,2},{2,0},{1,3},{3,1},{4,6},{6,4},{5,7},{7,5},{8,10},{10,8},{9,1... | collective-permute-start | bytes 196616 | tf_op jit(solution)/shard_map/ppermute | solution.py:239
  33.5 1.3 %collective-permute-start.5 = (f32[2,2,32,128]{3,2,1,0:T(8,128)S(1)}, f32[2,2,32,128]{3,2,1,0:T(8,128)S(1)}, u32[]{:S(2)}, u32[]{:S(2)}) collective-permute-start(f32[2,2,32,128]{3,2,1,0:T(8,128)S(1)} %get-tuple-element.14), channel_id=1, source_target_pairs={{0,1},{1,0},{2,3},{3,2},{4,5},{5,4},{6,7},{7,6},{8,9},{9,8},{10,11... | collective-permute-start | bytes 196616 | tf_op jit(solution)/shard_map/ppermute | solution.py:239
  34.9 16.2 %collective-permute-start.8 = (f16[264,128]{1,0:T(8,128)(2,1)S(1)}, f16[264,128]{1,0:T(8,128)(2,1)S(1)}, u32[]{:S(2)}, u32[]{:S(2)}) collective-permute-start(f16[264,128]{1,0:T(8,128)(2,1)S(1)} %convert_element_type.53), channel_id=1, source_target_pairs={{0,12},{4,8},{8,4},{12,0},{1,13},{5,9},{9,5},{13,1},{2,14},{6,10},... | collective-permute-start | bytes 202760 | tf_op jit(solution)/shard_map/ppermute | solution.py:239
  37.4 13.7 %collective-permute-start.7 = (f16[264,128]{1,0:T(8,128)(2,1)S(1)}, f16[264,128]{1,0:T(8,128)(2,1)S(1)}, u32[]{:S(2)}, u32[]{:S(2)}) collective-permute-start(f16[264,128]{1,0:T(8,128)(2,1)S(1)} %convert_element_type.53), channel_id=1, source_target_pairs={{0,8},{4,12},{8,0},{12,4},{1,9},{5,13},{9,1},{13,5},{2,10},{6,14},... | collective-permute-start | bytes 202760 | tf_op jit(solution)/shard_map/ppermute | solution.py:239
  37.4 13.7 %collective-permute-start.6 = (f16[264,128]{1,0:T(8,128)(2,1)S(1)}, f16[264,128]{1,0:T(8,128)(2,1)S(1)}, u32[]{:S(2)}, u32[]{:S(2)}) collective-permute-start(f16[264,128]{1,0:T(8,128)(2,1)S(1)} %convert_element_type.53), channel_id=1, source_target_pairs={{0,4},{4,0},{8,12},{12,8},{1,5},{5,1},{9,13},{13,9},{2,6},{6,2},{1... | collective-permute-start | bytes 202760 | tf_op jit(solution)/shard_map/ppermute | solution.py:239
  63.9 2.0 %collective-permute-start.9 = (f32[2,32,2048]{2,1,0:T(8,128)S(1)}, f32[2,32,2048]{2,1,0:T(8,128)S(1)}, u32[]{:S(2)}, u32[]{:S(2)}) collective-permute-start(f32[2,32,2048]{2,1,0:T(8,128)S(1)} %slice_bitcast_fusion), channel_id=1, source_target_pairs={{0,1},{1,0},{2,3},{3,2},{4,5},{5,4},{6,7},{7,6},{8,9},{9,8},{10,11... | collective-permute-start | bytes 1572872 | tf_op jit(solution)/shard_map/ppermute | solution.py:239
  65.9 5.6 %collective-permute-start.10 = (bf16[32,2048]{1,0:T(8,128)(2,1)S(1)}, bf16[32,2048]{1,0:T(8,128)(2,1)S(1)}, u32[]{:S(2)}, u32[]{:S(2)}) collective-permute-start(bf16[32,2048]{1,0:T(8,128)(2,1)S(1)} %fusion.7), channel_id=1, source_target_pairs={{0,16},{16,0},{1,17},{17,1},{2,18},{18,2},{3,19},{19,3},{4,20},{20... | collective-permute-start | bytes 393224 | tf_op jit(solution)/shard_map/ppermute | solution.py:239
  71.6 5.0 %collective-permute-start.11 = (bf16[32,2048]{1,0:T(8,128)(2,1)S(1)}, bf16[32,2048]{1,0:T(8,128)(2,1)S(1)}, u32[]{:S(2)}, u32[]{:S(2)}) collective-permute-start(bf16[32,2048]{1,0:T(8,128)(2,1)S(1)} %fusion.8), channel_id=1, source_target_pairs={{0,2},{2,0},{1,3},{3,1},{4,6},{6,4},{5,7},{7,5},{8,10},{10,8},{9,1... | collective-permute-start | bytes 393224 | tf_op jit(solution)/shard_map/ppermute | solution.py:239
  77.5 1.3 %collective-permute-start.12 = (f32[32,512]{1,0:T(8,128)S(1)}, f32[32,512]{1,0:T(8,128)S(1)}, u32[]{:S(2)}, u32[]{:S(2)}) collective-permute-start(f32[32,512]{1,0:T(8,128)S(1)} %slice_add_fusion), channel_id=1, source_target_pairs={{0,1},{1,0},{2,3},{3,2},{4,5},{5,4},{6,7},{7,6},{8,9},{9,8},{10,11... | collective-permute-start | bytes 196616 | tf_op jit(solution)/shard_map/ppermute | solution.py:239
  78.8 6.8 %collective-permute-start.15 = (f32[32,512]{1,0:T(8,128)S(1)}, f32[32,512]{1,0:T(8,128)S(1)}, u32[]{:S(2)}, u32[]{:S(2)}) collective-permute-start(f32[32,512]{1,0:T(8,128)S(1)} %fusion.17), channel_id=1, source_target_pairs={{0,12},{4,8},{8,4},{12,0},{1,13},{5,9},{9,5},{13,1},{2,14},{6,10},... | collective-permute-start | bytes 196616 | tf_op jit(solution)/shard_map/ppermute | solution.py:239
  81.3 6.3 %collective-permute-start.14 = (f32[32,512]{1,0:T(8,128)S(1)}, f32[32,512]{1,0:T(8,128)S(1)}, u32[]{:S(2)}, u32[]{:S(2)}) collective-permute-start(f32[32,512]{1,0:T(8,128)S(1)} %fusion.17), channel_id=1, source_target_pairs={{0,8},{4,12},{8,0},{12,4},{1,9},{5,13},{9,1},{13,5},{2,10},{6,14},... | collective-permute-start | bytes 196616 | tf_op jit(solution)/shard_map/ppermute | solution.py:239
  81.3 6.3 %collective-permute-start.13 = (f32[32,512]{1,0:T(8,128)S(1)}, f32[32,512]{1,0:T(8,128)S(1)}, u32[]{:S(2)}, u32[]{:S(2)}) collective-permute-start(f32[32,512]{1,0:T(8,128)S(1)} %fusion.17), channel_id=1, source_target_pairs={{0,4},{4,0},{8,12},{12,8},{1,5},{5,1},{9,13},{13,9},{2,6},{6,2},{1... | collective-permute-start | bytes 196616 | tf_op jit(solution)/shard_map/ppermute | solution.py:239
